TPU v7x, 32 devices: a whole 2x2x4 slice. The times are simulated.
32 devices in a mesh: sample: 2 (over x), head: 4 (over z), group: 4 (over y, core).
Axes of the slice: x: 2, y: 2, z: 4, core: 2. Of those that a mesh axis runs over, the one named last changes fastest.
Arguments:
- queries: bfloat16 [4, 4, 128, 8192], P('group', 'sample', None, 'head'), may hold values from -6 to 6
- kv_comp: bfloat16 [2, 4, 4, 128, 1024], P(None, 'group', 'sample', None, 'head'), may hold values from -6 to 6
- kv_prefix: bfloat16 [2, 4, 512, 1024], P(None, 'group', ('sample', 'head')), may hold values from -6 to 6
- grad_out: bfloat16 [4, 4, 128, 8192], P('group', 'sample', None, 'head'), may hold values from -6 to 6
- prompt_len: int32 [4], P('group'), may hold values from 128 to 512, as said below
- comp_len: int32 [4, 4], P('group', 'sample'), may hold values from 32 to 128, as said below
Outputs:
- attended: bfloat16 [4, 4, 128, 8192], P('group', 'sample', None, 'head')
- grad_queries: bfloat16 [4, 4, 128, 8192], P('group', 'sample', None, 'head')
- grad_comp: bfloat16 [2, 4, 4, 128, 1024], P(None, 'group', 'sample', None, 'head')
- grad_prefix: bfloat16 [2, 4, 512, 1024], P(None, 'group', ('sample', 'head'))
Inputs may be any that keep to these rules, and one draw needn't show every extreme that they name: `prompt_len`: one group has exactly 512 prompt tokens and another exactly 128. `comp_len`: in every group one rollout has exactly 128 completion tokens and another exactly 32.
All inputs are finite; a program needn't handle non-finite values.
Results may differ from a plain program's by a relative error of at most 0.014.
Values may be sent and summed in bfloat16 or wider, within the bound.
A program may use at most 128 MiB of HBM per device.

v0:
```python
import jax
import jax.numpy as jnp
from jax import lax
from jax.sharding import PartitionSpec as P

DH = 128


def body(queries, kv_comp, kv_prefix, grad_out, prompt_len, comp_len):
    feature_dev = kv_comp.shape[4]
    kv_local = feature_dev // DH
    repeats = queries.shape[3] // feature_dev
    rollouts = queries.shape[1]
    comp_rows = queries.shape[2]
    sample_count = lax.axis_size("sample")
    head_count = lax.axis_size("head")
    regrouped = lax.all_to_all(kv_prefix, "head", split_axis=3, concat_axis=2, tiled=True)
    own_prefix = lax.all_gather(regrouped, "sample", axis=2, tiled=True)
    prefix_rows = own_prefix.shape[2]
    softmax_scale = 1.0 / DH**0.5
    query_all = queries[0].reshape(rollouts, comp_rows, kv_local, repeats, DH)
    grad_all = grad_out[0].reshape(rollouts, comp_rows, kv_local, repeats, DH)
    keys_comp = kv_comp[0, 0].reshape(rollouts, comp_rows, kv_local, DH)
    values_comp = kv_comp[1, 0].reshape(rollouts, comp_rows, kv_local, DH)
    keys_prefix = own_prefix[0, 0].reshape(prefix_rows, kv_local, DH)
    values_prefix = own_prefix[1, 0].reshape(prefix_rows, kv_local, DH)
    prefix_live = jnp.arange(prefix_rows, dtype=jnp.int32) < prompt_len[0]
    positions = jnp.arange(comp_rows, dtype=jnp.int32)
    causal = positions[None, :] <= positions[:, None]
    query_live = (positions[None, :] < comp_len[0][:, None]).astype(jnp.float32)[:, None, :, None]
    attended_parts = []
    grad_query_parts = []
    grad_key_parts = []
    grad_value_parts = []
    prefix_weights = []
    prefix_slopes = []
    for kv_slot in range(kv_local):
        query_one = query_all[:, :, kv_slot]
        grad_one = grad_all[:, :, kv_slot]
        key_prefix_one = keys_prefix[:, kv_slot]
        value_prefix_one = values_prefix[:, kv_slot]
        key_comp_one = keys_comp[:, :, kv_slot]
        value_comp_one = values_comp[:, :, kv_slot]
        scores_prefix = (
            jnp.einsum(
                "rtjd,pd->rjtp", query_one, key_prefix_one, preferred_element_type=jnp.float32
            )
            * softmax_scale
        )
        scores_comp = (
            jnp.einsum(
                "rtjd,rud->rjtu", query_one, key_comp_one, preferred_element_type=jnp.float32
            )
            * softmax_scale
        )
        scores_prefix = jnp.where(prefix_live, scores_prefix, -jnp.inf)
        scores_comp = jnp.where(causal, scores_comp, -jnp.inf)
        row_max = jnp.maximum(jnp.max(scores_prefix, axis=-1), jnp.max(scores_comp, axis=-1))
        exp_total = jnp.sum(jnp.exp(scores_prefix - row_max[..., None]), axis=-1) + jnp.sum(
            jnp.exp(scores_comp - row_max[..., None]), axis=-1
        )
        log_total = row_max + jnp.log(exp_total)
        weights_prefix32 = jnp.exp(scores_prefix - log_total[..., None]) * query_live
        weights_comp32 = jnp.exp(scores_comp - log_total[..., None]) * query_live
        weights_prefix = weights_prefix32.astype(jnp.bfloat16)
        weights_comp = weights_comp32.astype(jnp.bfloat16)
        attended_one = (
            jnp.einsum(
                "rjtp,pd->rtjd",
                weights_prefix,
                value_prefix_one,
                preferred_element_type=jnp.float32,
            )
            + jnp.einsum(
                "rjtu,rud->rtjd", weights_comp, value_comp_one, preferred_element_type=jnp.float32
            )
        ).astype(jnp.bfloat16)
        row_dot = jnp.sum(grad_one.astype(jnp.float32) * attended_one.astype(jnp.float32), axis=-1)
        row_dot = jnp.transpose(row_dot, (0, 2, 1))[..., None]
        slope_prefix = (
            weights_prefix32
            * (
                jnp.einsum(
                    "rtjd,pd->rjtp", grad_one, value_prefix_one, preferred_element_type=jnp.float32
                )
                - row_dot
            )
        ).astype(jnp.bfloat16)
        slope_comp = (
            weights_comp32
            * (
                jnp.einsum(
                    "rtjd,rud->rjtu", grad_one, value_comp_one, preferred_element_type=jnp.float32
                )
                - row_dot
            )
        ).astype(jnp.bfloat16)
        grad_query_one = (
            softmax_scale
            * (
                jnp.einsum(
                    "rjtp,pd->rtjd",
                    slope_prefix,
                    key_prefix_one,
                    preferred_element_type=jnp.float32,
                )
                + jnp.einsum(
                    "rjtu,rud->rtjd", slope_comp, key_comp_one, preferred_element_type=jnp.float32
                )
            )
        ).astype(jnp.bfloat16)
        grad_key_one = (
            softmax_scale
            * jnp.einsum(
                "rjtu,rtjd->rud", slope_comp, query_one, preferred_element_type=jnp.float32
            )
        ).astype(jnp.bfloat16)
        grad_value_one = jnp.einsum(
            "rjtu,rtjd->rud", weights_comp, grad_one, preferred_element_type=jnp.float32
        ).astype(jnp.bfloat16)
        attended_parts.append(attended_one)
        grad_query_parts.append(grad_query_one)
        grad_key_parts.append(grad_key_one)
        grad_value_parts.append(grad_value_one)
        prefix_weights.append(weights_prefix)
        prefix_slopes.append(slope_prefix)
    attended = jnp.stack(attended_parts, axis=2).reshape(
        1, rollouts, comp_rows, kv_local * repeats * DH
    )
    grad_queries = jnp.stack(grad_query_parts, axis=2).reshape(
        1, rollouts, comp_rows, kv_local * repeats * DH
    )
    grad_comp = jnp.stack(
        [jnp.stack(grad_key_parts, axis=2), jnp.stack(grad_value_parts, axis=2)]
    ).reshape(2, 1, rollouts, comp_rows, feature_dev)
    pieces = []
    for kv_slot in range(kv_local):
        slope_rows = prefix_slopes[kv_slot]
        weight_rows = prefix_weights[kv_slot]
        key_grad = softmax_scale * jnp.einsum(
            "rjtp,rtjd->pd",
            slope_rows,
            query_all[:, :, kv_slot],
            preferred_element_type=jnp.float32,
        )
        value_grad = jnp.einsum(
            "rjtp,rtjd->pd",
            weight_rows,
            grad_all[:, :, kv_slot],
            preferred_element_type=jnp.float32,
        )
        pieces.append(jnp.stack([key_grad, value_grad], axis=1))
    full_term = jnp.concatenate(pieces, axis=2)
    block_rows = prefix_rows // (sample_count * head_count)
    reordered = jnp.transpose(
        full_term.reshape(sample_count, head_count, block_rows, 2, feature_dev), (1, 0, 2, 3, 4)
    ).reshape(prefix_rows, 2, feature_dev)
    moved_rows = lax.all_to_all(reordered, "head", split_axis=0, concat_axis=2, tiled=True)
    returned = lax.psum_scatter(moved_rows, "sample", scatter_dimension=0, tiled=True).astype(
        jnp.bfloat16
    )
    grad_prefix = jnp.transpose(returned, (1, 0, 2))[:, None]
    return (attended, grad_queries, grad_comp, grad_prefix)


def solution(mesh):
    return jax.shard_map(
        body,
        mesh=mesh,
        in_specs=(
            P("group", "sample", None, "head"),
            P(None, "group", "sample", None, "head"),
            P(None, "group", ("sample", "head"), None),
            P("group", "sample", None, "head"),
            P("group"),
            P("group", "sample"),
        ),
        out_specs=(
            P("group", "sample", None, "head"),
            P("group", "sample", None, "head"),
            P(None, "group", "sample", None, "head"),
            P(None, "group", ("sample", "head"), None),
        ),
        check_vma=False,
    )
```

profile of v0, /device:TPU:0, one launch (start us, length us, event | category | flops | bytes accessed | tf_op | source)
XLA Modules:
  0.0 123.9 jit_solution(7865120312606395615)
XLA Ops:
  0.7 1.4 %copy.233 = bf16[2,1,64,1024]{2,0,1,3:T(2,128)(2,1)S(1)} copy(bf16[2,1,64,1024]{3,2,1,0:T(8,128)(2,1)} %param.8) | data formatting | bytes 524288 | tf_op args[2]
  3.1 6.3 %all-to-all-start = ((bf16[4,2,16384]{2,1,0:T(2,128)(2,1)}), bf16[4,2,16384]{2,1,0:T(2,128)(2,1)S(1)}, u32[]{:S(2)}, u32[]{:S(2)}) async-start(bf16[4,2,16384]{2,1,0:T(2,128)(2,1)} %reshape.112), calls=%async_computation | async-start | bytes 524288 | tf_op jit(solution)/shard_map/all_to_all | solution.py:17
  9.5 1.6 %copy.238 = bf16[1,2,128,2048]{2,3,1,0:T(8,128)(2,1)S(1)} copy(bf16[1,2,128,2048]{3,2,1,0:T(8,128)(2,1)} %param.6) | data formatting | bytes 2097152 | tf_op args[0]
  21.7 1.5 %copy.348 = bf16[2,1,64,4,256]{4,3,2,0,1:T(4,128)(2,1)S(1)} copy(bf16[2,1,64,4,256]{2,0,4,3,1:T(2,128)(2,1)} %bitcast.369) | data formatting | bytes 524288 | tf_op jit(solution)/shard_map/all_to_all | solution.py:17
  23.2 8.4 %all_gather.3 = bf16[2,1,512,256]{3,2,0,1:T(8,128)(2,1)S(1)} all-gather(bf16[2,1,256,256]{3,2,0,1:T(8,128)(2,1)S(1)} %bitcast.385), channel_id=1, replica_groups=mesh['sample'=2,'head'=4,'group'=4] {'sample'}, dimensions={2}, use_global_device_ids=true | all-gather | bytes 786432 | tf_op jit(solution)/shard_map/all_gather | solution.py:18
  34.4 1.6 %fusion.9 = (f32[2,8,128]{2,1,0:T(8,128)S(1)}, f32[2,8,128]{2,1,0:T(8,128)S(1)}, f32[512,2,128,8]{2,0,3,1:T(8,128)S(1)}) fusion(f32[512,2,128,8]{2,0,3,1:T(8,128)S(1)} %get-tuple-element.35, f32[2,8,128]{2,1,0:T(8,128)S(1)} %max.20, pred[512]{0:T(512)(128)(4,1)S(1)} %copy-done.30, bf16[2,128,2,8,128]{1,4,3,2,0:T(8,128)(2,1)S(1)} %bitcast.351, ...), kind=kOutput, calls=%fused_computation.17 | convolution fusion | flops 275771392 | bytes 9069056 | tf_op jit(solution)/shard_map/rtjd,pd->rjtp/dot_general | solution.py:45
  37.4 3.8 %fusion.12 = (bf16[2,8,128,512]{2,3,1,0:T(8,128)(2,1)}, bf16[2,8,128,512]{2,3,1,0:T(8,128)(2,1)}) fusion(f32[512,2,128,8]{2,0,3,1:T(8,128)S(1)} %get-tuple-element.35, f32[2,128]{1,0:T(2,128)S(1)} %copy-done.28, f32[2,8,128]{2,1,0:T(8,128)S(1)} %get-tuple-element.43, pred[512]{0:T(512)(128)(4,1)S(1)} %copy-done.31, f32[2,8,128]{2,1,0:T(8,128)S(1)} %get-tuple-element.42, ...), kind=kLoop, calls=%fused_computation.22 | loop fusion | flops 10485760 | bytes 12600832 | tf_op jit(solution)/shard_map/convert_element_type | solution.py:65
  41.2 1.3 %fusion.84 = f32[2,8,128,128]{2,3,1,0:T(8,128)} fusion(f32[2,8,128,128]{2,3,1,0:T(8,128)S(1)} %get-tuple-element.40, f32[2,8,128]{2,1,0:T(8,128)S(1)} %get-tuple-element.42, f32[2,128]{1,0:T(2,128)S(1)} %copy-done.28, bf16[2,128,2,128]{1,3,2,0:T(8,128)(2,1)S(1)} %bitcast.380), kind=kOutput, calls=%fused_computation.110 | convolution fusion | flops 67895296 | bytes 2171904 | tf_op jit(solution)/shard_map/rjtu,rud->rtjd/dot_general | solution.py:74
  42.5 1.4 %fusion.87 = f32[2,8,128,128]{2,3,1,0:T(8,128)} fusion(f32[2,8,128,128]{2,3,1,0:T(8,128)S(1)} %get-tuple-element.37, f32[2,128]{1,0:T(2,128)S(1)} %copy-done.28, f32[2,8,128]{2,1,0:T(8,128)S(1)} %get-tuple-element.43, bf16[2,128,2,128]{1,3,2,0:T(8,128)(2,1)S(1)} %bitcast.381), kind=kOutput, calls=%fused_computation.111 | convolution fusion | flops 67895296 | bytes 2171904 | tf_op jit(solution)/shard_map/rjtu,rud->rtjd/dot_general | solution.py:74
  43.9 1.8 %copy.242 = bf16[1,1,512,256]{2,3,1,0:T(8,128)(2,1)} copy(bf16[1,1,512,256]{3,2,0,1:T(8,128)(2,1)} %get-tuple-element.28) | data formatting | bytes 524288 | tf_op jit(solution)/shard_map/slice | solution.py:26
  45.7 2.5 %fusion.35 = bf16[2,8,128,128]{2,3,1,0:T(8,128)(2,1)S(1)} fusion(f32[2,8,128,128]{2,3,1,0:T(8,128)} %fusion.84, bf16[2,8,128,512]{2,3,1,0:T(8,128)(2,1)} %get-tuple-element.33, bf16[512,2,128]{0,2,1:T(8,128)(2,1)} %bitcast.386), kind=kOutput, calls=%fused_computation.53 | convolution fusion | flops 268959744 | bytes 3801088 | tf_op jit(solution)/shard_map/rjtp,pd->rtjd/dot_general | solution.py:68
  48.5 3.4 %multiply_reduce_fusion.1 = (f32[2,128,8]{1,2,0:T(8,128)S(1)}, f32[2,128,8]{1,2,0:T(8,128)S(1)}, bf16[2,8,128,128]{2,3,1,0:T(8,128)(2,1)}) fusion(bf16[2,128,2,8,128]{1,4,3,2,0:T(8,128)(2,1)} %bitcast.355, bf16[2,8,128,128]{2,3,1,0:T(8,128)(2,1)S(1)} %fusion.35, f32[2,8,128,128]{2,3,1,0:T(8,128)S(1)} %copy-done.10, ...), kind=kOutput, calls=%fused_computation.84 | convolution fusion | flops 271052800 | bytes 5390336 | tf_op jit(solution)/shard_map/rjtp,pd->rtjd/dot_general | solution.py:68
  52.0 1.5 %fusion.3 = bf16[2,8,128,512]{2,3,1,0:T(8,128)(2,1)S(1)} fusion(f32[512,2,128,8]{2,0,3,1:T(8,128)S(1)} %copy-done.1, f32[2,8,128]{2,1,0:T(8,128)S(1)} %bitcast.394, f32[2,128]{1,0:T(2,128)S(1)} %copy-done.29, f32[2,8,128]{2,1,0:T(8,128)S(1)} %get-tuple-element.43, pred[512]{0:T(512)(128)(4,1)S(1)} %copy-done.32, bf16[512,2,128]{0,2,1:T(8,128)(2,1)S(1)} %bitcast.388, ...), kind=kOutput, calls=%fused_computation.5 | convolution fusion | flops 275775488 | bytes 6964736 | tf_op jit(solution)/shard_map/rtjd,pd->rjtp/dot_general | solution.py:83
  53.6 1.5 %fusion.33 = bf16[2,8,128,128]{2,3,1,0:T(8,128)(2,1)} fusion(f32[2,8,128,128]{2,3,1,0:T(8,128)S(1)} %get-tuple-element.37, f32[2,8,128]{2,1,0:T(8,128)S(1)} %bitcast.395, f32[2,128]{1,0:T(2,128)S(1)} %copy-done.29, f32[2,8,128]{2,1,0:T(8,128)S(1)} %get-tuple-element.43, bf16[2,128,2,128]{1,3,2,0:T(8,128)(2,1)S(1)} %bitcast.382, ...), kind=kOutput, calls=%fused_computation.51 | convolution fusion | flops 68419584 | bytes 2180096 | tf_op jit(solution)/shard_map/rtjd,rud->rjtu/dot_general | solution.py:92
  55.0 1.5 %fusion.1 = bf16[2,8,128,512]{2,3,1,0:T(8,128)(2,1)S(1)} fusion(f32[512,2,128,8]{2,0,3,1:T(8,128)S(1)} %copy-done.3, f32[2,8,128]{2,1,0:T(8,128)S(1)} %bitcast.392, f32[2,8,128]{2,1,0:T(8,128)S(1)} %get-tuple-element.42, f32[2,128]{1,0:T(2,128)S(1)} %copy-done.29, pred[512]{0:T(512)(128)(4,1)S(1)} %copy-done.32, bf16[512,2,128]{0,2,1:T(8,128)(2,1)S(1)} %bitcast.389, ...), kind=kOutput, calls=%fused_computation.2 | convolution fusion | flops 275775488 | bytes 6964736 | tf_op jit(solution)/shard_map/rtjd,pd->rjtp/dot_general | solution.py:83
  56.6 1.2 fusion.32
  63.6 1.8 %copy.292 = f32[512,2,256]{2,1,0:T(2,128)} copy(f32[512,2,256]{2,0,1:T(8,128)S(1)} %bitcast.364) | data formatting | bytes 2097152 | tf_op jit(solution)/shard_map/reshape | solution.py:157
  65.4 4.8 %all-to-all-start.1 = ((f32[512,2,256]{2,1,0:T(2,128)}), f32[512,2,256]{2,1,0:T(2,128)S(1)}, u32[]{:S(2)}, u32[]{:S(2)}) async-start(f32[512,2,256]{2,1,0:T(2,128)} %copy.292), calls=%async_computation.1 | async-start | bytes 2097152 | tf_op jit(solution)/shard_map/all_to_all | solution.py:158
  73.0 2.1 %fusion.38 = bf16[2,128,1,8,128]{1,4,3,0,2:T(8,128)(2,1)S(1)} fusion(f32[2,8,128,128]{2,3,1,0:T(8,128)S(1)} %fusion.89, bf16[2,8,128,512]{2,3,1,0:T(8,128)(2,1)} %copy-done.12, bf16[512,2,128]{0,2,1:T(8,128)(2,1)S(1)} %bitcast.374), kind=kOutput, calls=%fused_computation.56 | convolution fusion | flops 269221888 | bytes 3801088 | tf_op jit(solution)/shard_map/rjtp,pd->rtjd/dot_general | solution.py:101
  75.3 2.1 %fusion.39 = bf16[2,128,1,8,128]{1,4,3,0,2:T(8,128)(2,1)S(1)} fusion(f32[2,8,128,128]{2,3,1,0:T(8,128)S(1)} %fusion.90, bf16[2,8,128,512]{2,3,1,0:T(8,128)(2,1)} %copy-done.11, bf16[512,2,128]{0,2,1:T(8,128)(2,1)S(1)} %bitcast.375), kind=kOutput, calls=%fused_computation.57 | convolution fusion | flops 269221888 | bytes 3801088 | tf_op jit(solution)/shard_map/rjtp,pd->rtjd/dot_general | solution.py:101
  77.7 1.3 %copy.297 = bf16[1,2,128,2048]{3,2,1,0:T(8,128)(2,1)} copy(bf16[1,2,128,2048]{2,3,1,0:T(8,128)(2,1)S(1)} %bitcast.365) | data formatting | bytes 2097152
  79.2 1.3 %copy.296 = bf16[1,2,128,2048]{3,2,1,0:T(8,128)(2,1)} copy(bf16[1,2,128,2048]{2,3,1,0:T(8,128)(2,1)S(1)} %bitcast.366) | data formatting | bytes 2097152
  80.5 13.9 %all-to-all-done.1 = f32[512,2,256]{2,1,0:T(2,128)S(1)} async-done(((f32[512,2,256]{2,1,0:T(2,128)}), f32[512,2,256]{2,1,0:T(2,128)S(1)}, u32[]{:S(2)}, u32[]{:S(2)}) %all-to-all-start.1) | async-done | bytes 1048608 | tf_op jit(solution)/shard_map/all_to_all | solution.py:158
  95.5 27.4 %all-reduce.2 = bf16[128,2,1024]{2,1,0:T(2,128)(2,1)S(1)} all-reduce(f32[128,2,1024]{2,1,0:T(2,128)S(1)} %copy.295), channel_id=2, replica_groups=mesh['sample'=2,'head'=4,'group'=4] {'sample'}, use_global_device_ids=true, to_apply=%region_10.11.clone | all-reduce | flops 262144 | bytes 1572864
  (123 shorter events, 25.6 us)
Async XLA Ops:
  0.6 10.5 %copy-start.25 = (bf16[2,1,2,128,256]{4,3,2,1,0:T(8,128)(2,1)S(1)}, bf16[2,1,2,128,256]{4,3,2,1,0:T(8,128)(2,1)}, u32[]{:S(2)}) copy-start(bf16[2,1,2,128,256]{4,3,2,1,0:T(8,128)(2,1)} %param.7) | copy-start | bytes 786436
  0.6 11.3 %copy-start.18 = (bf16[1,2,128,2048]{3,2,1,0:T(8,128)(2,1)S(1)}, bf16[1,2,128,2048]{3,2,1,0:T(8,128)(2,1)}, u32[]{:S(2)}) copy-start(bf16[1,2,128,2048]{3,2,1,0:T(8,128)(2,1)} %param.9) | copy-start | bytes 3145732
  3.1 17.4 %all-to-all-start = ((bf16[4,2,16384]{2,1,0:T(2,128)(2,1)}), bf16[4,2,16384]{2,1,0:T(2,128)(2,1)S(1)}, u32[]{:S(2)}, u32[]{:S(2)}) async-start(bf16[4,2,16384]{2,1,0:T(2,128)(2,1)} %reshape.112), calls=%async_computation | async-start | bytes 524288 | tf_op jit(solution)/shard_map/all_to_all | solution.py:17
  12.6 3.1 %copy-start.33 = (s32[1,2]{1,0:T(1,128)S(1)}, s32[1,2]{1,0:T(1,128)}, u32[]{:S(2)}) copy-start(s32[1,2]{1,0:T(1,128)} %param.11) | copy-start | bytes 28
  12.6 4.4 %copy-start.20 = (bf16[1,1,2,128,256]{4,3,2,1,0:T(8,128)(2,1)S(1)}, bf16[1,1,2,128,256]{4,3,2,1,0:T(8,128)(2,1)}, u32[]{:S(2)}) copy-start(bf16[1,1,2,128,256]{4,3,2,1,0:T(8,128)(2,1)} %get-tuple-element.30) | copy-start | bytes 393220
  12.6 5.1 %copy-start.34 = (u32[32]{0:T(128)S(1)}, u32[32]{0:T(128)}, u32[]{:S(2)}) copy-start(u32[32]{0:T(128)} %constant.18) | copy-start | bytes 388
  20.5 13.1 %copy-start.30 = (pred[512]{0:T(512)(128)(4,1)S(1)}, pred[512]{0:T(512)(128)(4,1)}, u32[]{:S(2)}) copy-start(pred[512]{0:T(512)(128)(4,1)} %iota_compare_fusion.1) | copy-start | bytes 1540
  21.7 12.7 %copy-start.26 = (f32[2,8,128]{2,1,0:T(8,128)S(1)}, f32[2,8,128]{2,1,0:T(8,128)}, u32[]{:S(2)}) copy-start(f32[2,8,128]{2,1,0:T(8,128)} %get-tuple-element.36) | copy-start | bytes 24580
  36.0 5.2 %copy-start.2 = (f32[512,2,128,8]{2,0,3,1:T(8,128)}, f32[512,2,128,8]{2,0,3,1:T(8,128)S(1)}, u32[]{:S(2)}) copy-start(f32[512,2,128,8]{2,0,3,1:T(8,128)S(1)} %get-tuple-element.38) | copy-start | bytes 12582916
  37.3 3.9 %copy-start.16 = (bf16[1,1,2,128,256]{3,4,2,1,0:T(8,128)(2,1)S(1)}, bf16[1,1,2,128,256]{3,4,2,1,0:T(8,128)(2,1)}, u32[]{:S(2)}) copy-start(bf16[1,1,2,128,256]{3,4,2,1,0:T(8,128)(2,1)} %copy.371) | copy-start | bytes 393220
  45.7 6.3 %copy-start.1 = (f32[512,2,128,8]{2,0,3,1:T(8,128)S(1)}, f32[512,2,128,8]{2,0,3,1:T(8,128)}, u32[]{:S(2)}) copy-start(f32[512,2,128,8]{2,0,3,1:T(8,128)} %copy-done) | copy-start | bytes 12582916
  45.7 6.3 %copy-start.5 = (bf16[1,2,128,2048]{2,3,1,0:T(8,128)(2,1)S(1)}, bf16[1,2,128,2048]{2,3,1,0:T(8,128)(2,1)}, u32[]{:S(2)}) copy-start(bf16[1,2,128,2048]{2,3,1,0:T(8,128)(2,1)} %copy-done.4) | copy-start | bytes 3145732
  45.7 6.3 %copy-start.19 = (bf16[1,1,512,256]{2,3,1,0:T(8,128)(2,1)S(1)}, bf16[1,1,512,256]{2,3,1,0:T(8,128)(2,1)}, u32[]{:S(2)}) copy-start(bf16[1,1,512,256]{2,3,1,0:T(8,128)(2,1)} %copy.242) | copy-start | bytes 786436
  45.7 6.3 %copy-start.29 = (f32[2,128]{1,0:T(2,128)S(1)}, f32[2,128]{1,0:T(2,128)}, u32[]{:S(2)}) copy-start(f32[2,128]{1,0:T(2,128)} %compare_convert_fusion) | copy-start | bytes 3076
  45.7 6.3 %copy-start.32 = (pred[512]{0:T(512)(128)(4,1)S(1)}, pred[512]{0:T(512)(128)(4,1)}, u32[]{:S(2)}) copy-start(pred[512]{0:T(512)(128)(4,1)} %iota_compare_fusion.1) | copy-start | bytes 1540
  48.2 3.7 %copy-start.8 = (bf16[2,8,128,128]{2,3,1,0:T(8,128)(2,1)}, bf16[2,8,128,128]{2,3,1,0:T(8,128)(2,1)S(1)}, u32[]{:S(2)}) copy-start(bf16[2,8,128,128]{2,3,1,0:T(8,128)(2,1)S(1)} %fusion.35) | copy-start | bytes 1572868
  53.6 7.8 %copy-start.12 = (bf16[2,8,128,512]{2,3,1,0:T(8,128)(2,1)}, bf16[2,8,128,512]{2,3,1,0:T(8,128)(2,1)S(1)}, u32[]{:S(2)}) copy-start(bf16[2,8,128,512]{2,3,1,0:T(8,128)(2,1)S(1)} %fusion.3) | copy-start | bytes 6291460
  56.6 5.7 %copy-start.11 = (bf16[2,8,128,512]{2,3,1,0:T(8,128)(2,1)}, bf16[2,8,128,512]{2,3,1,0:T(8,128)(2,1)S(1)}, u32[]{:S(2)}) copy-start(bf16[2,8,128,512]{2,3,1,0:T(8,128)(2,1)S(1)} %fusion.1) | copy-start | bytes 6291460
  56.6 3.2 %copy-start.24 = (bf16[2,128,8,128]{1,3,2,0:T(8,128)(2,1)S(1)}, bf16[2,128,8,128]{1,3,2,0:T(8,128)(2,1)}, u32[]{:S(2)}) copy-start(bf16[2,128,8,128]{1,3,2,0:T(8,128)(2,1)} %get-tuple-element.26) | copy-start | bytes 1572868
  63.5 6.7 %copy-start.14 = (bf16[2,8,128,128]{2,3,1,0:T(8,128)(2,1)S(1)}, bf16[2,8,128,128]{2,3,1,0:T(8,128)(2,1)}, u32[]{:S(2)}) copy-start(bf16[2,8,128,128]{2,3,1,0:T(8,128)(2,1)} %fusion.33) | copy-start | bytes 1572868
  63.5 7.0 %copy-start.15 = (bf16[2,8,128,128]{2,3,1,0:T(8,128)(2,1)S(1)}, bf16[2,8,128,128]{2,3,1,0:T(8,128)(2,1)}, u32[]{:S(2)}) copy-start(bf16[2,8,128,128]{2,3,1,0:T(8,128)(2,1)} %fusion.32) | copy-start | bytes 1572868
  65.4 29.1 %all-to-all-start.1 = ((f32[512,2,256]{2,1,0:T(2,128)}), f32[512,2,256]{2,1,0:T(2,128)S(1)}, u32[]{:S(2)}, u32[]{:S(2)}) async-start(f32[512,2,256]{2,1,0:T(2,128)} %copy.292), calls=%async_computation.1 | async-start | bytes 2097152 | tf_op jit(solution)/shard_map/all_to_all | solution.py:158
  75.3 3.7 %copy-start.9 = (bf16[2,8,128,128]{2,3,1,0:T(8,128)(2,1)S(1)}, bf16[2,8,128,128]{2,3,1,0:T(8,128)(2,1)}, u32[]{:S(2)}) copy-start(bf16[2,8,128,128]{2,3,1,0:T(8,128)(2,1)} %copy-done.8) | copy-start | bytes 1572868
  75.3 3.7 %copy-start.13 = (bf16[2,8,128,128]{2,3,1,0:T(8,128)(2,1)S(1)}, bf16[2,8,128,128]{2,3,1,0:T(8,128)(2,1)}, u32[]{:S(2)}) copy-start(bf16[2,8,128,128]{2,3,1,0:T(8,128)(2,1)} %get-tuple-element.41) | copy-start | bytes 1572868
  (13 other events, 28.4 us)
where the time goes:
time: 124 us
  blocking collectives  35.9 us (29%)
  matrix products  29.1 us (23%)
  local copies, waits for them, and re-layouts  23.6 us (19%)
  waiting for transfers between devices  13.9 us (11%)
  starting transfers between devices  11.1 us (9%)
  other arithmetic  7.54 us (6%)
  between operations  2.66 us (2%)
    unnamed x1, blocking collectives  27.4 us
    all_to_all x1, waiting for transfers between devices, body(): lax.all_to_all(reordered, 'head', split_axis=0, concat_axis=2, tiled=True)  13.9 us
    unnamed x82, local copies, waits for them, and re-layouts  12 us
    all_gather x1, blocking collectives, body(): own_prefix = lax.all_gather(regrouped, 'sample', axis=2, tiled=True)  8.44 us
    all_to_all x1, starting transfers between devices, body(): lax.all_to_all(kv_prefix, 'head', split_axis=3, concat_axis=2, tiled=True)  6.32 us
    dot_general x2, matrix products, body(): jnp.einsum('rjtp,pd->rtjd', weights_prefix, value_prefix_one, preferred_e...  5.93 us
    all_to_all x1, starting transfers between devices, body(): lax.all_to_all(reordered, 'head', split_axis=0, concat_axis=2, tiled=True)  4.82 us
    dot_general x2, matrix products, body(): jnp.einsum('rjtp,pd->rtjd', slope_prefix, key_prefix_one, preferred_eleme...  4.19 us
  transfers between devices with their start and end apart: 2, of which 1 were waited for; matrix products, arithmetic and copies ran while one was open for 16% of the time, Pallas kernels for 0%

commit v1 on v0

v1 whole, which is shorter than its diff:
```python
import functools

import jax
import jax.numpy as jnp
from jax import lax
from jax.experimental import pallas as pl
from jax.experimental.pallas import tpu as pltpu
from jax.sharding import PartitionSpec as P

DH = 128
NEG = -1e30
MESH = pl.DeviceIdType.MESH
SCALE = 1.0 / DH**0.5
EXP2_SCALE = SCALE * 1.4426950408889634
F32 = jnp.float32
BF16 = jnp.bfloat16
HEADS_TILE = 2


def dot(a, b, dims):
    return lax.dot_general(a, b, (dims, ((), ())), preferred_element_type=F32)


def kernel(
    samples,
    heads,
    plen_ref,
    clen_ref,
    q_ref,
    g_ref,
    kvc_ref,
    kvp_ref,
    att_ref,
    dq_ref,
    gc_ref,
    gp_ref,
    landed,
    keys,
    values,
    keys_t,
    values_t,
    acc_k,
    acc_v,
    outgoing,
    incoming,
    send_a,
    recv_a,
    send_b,
    recv_b,
):
    peers = samples * heads
    kv_local = kvc_ref.shape[4] // DH
    rollouts, comp_rows = q_ref.shape[1], q_ref.shape[2]
    repeats = q_ref.shape[3] // kvc_ref.shape[4]
    block_rows = kvp_ref.shape[2]
    prefix_rows = block_rows * peers
    all_rows = prefix_rows + comp_rows
    tiles = repeats // HEADS_TILE
    tile_rows = HEADS_TILE * comp_rows
    me = lax.axis_index("sample") * heads + lax.axis_index("head")

    def device(block):
        return {"sample": lax.div(block, heads), "head": lax.rem(block, heads)}

    def ahead(j):
        return lax.rem(me + j, peers)

    def behind(j):
        return lax.rem(me + peers - j, peers)

    def rows_of(block):
        return pl.ds(pl.multiple_of(block * block_rows, block_rows), block_rows)

    def gather_copy(kv, j, to, owner):
        head = lax.rem(to, heads)
        lanes = pl.ds(pl.multiple_of((head * kv_local + kv) * DH, DH), DH)
        return pltpu.make_async_remote_copy(
            src_ref=kvp_ref.at[:, 0, :, lanes],
            dst_ref=landed.at[kv, :, rows_of(owner), :],
            send_sem=send_a.at[kv, j],
            recv_sem=recv_a.at[kv, j],
            device_id=device(to),
            device_id_type=MESH,
        )

    def reduce_copy(kv, j, to, owner):
        return pltpu.make_async_remote_copy(
            src_ref=outgoing.at[kv, :, rows_of(to), :],
            dst_ref=incoming.at[kv, owner],
            send_sem=send_b.at[kv, j],
            recv_sem=recv_b.at[kv, j],
            device_id=device(to),
            device_id_type=MESH,
        )

    barrier = pltpu.get_barrier_semaphore()
    for j in range(1, peers):
        pl.semaphore_signal(barrier, inc=1, device_id=device(ahead(j)), device_id_type=MESH)
    pl.semaphore_wait(barrier, peers - 1)
    for kv in range(kv_local):
        for j in range(1, peers):
            gather_copy(kv, j, ahead(j), me).start()

    my_head = lax.rem(me, heads)
    for kv in range(kv_local):
        lanes = pl.ds(pl.multiple_of((my_head * kv_local + kv) * DH, DH), DH)
        landed[kv, :, rows_of(me), :] = kvp_ref[:, 0, :, lanes]

    row_id = lax.broadcasted_iota(jnp.int32, (comp_rows, comp_rows), 0)
    lane_id = lax.broadcasted_iota(jnp.int32, (comp_rows, comp_rows), 1)
    one_hot = jnp.where(row_id == lane_id, 1.0, 0.0).astype(BF16)
    causal = jnp.where(row_id <= lane_id, 0.0, NEG).astype(BF16)
    prefix_id = lax.broadcasted_iota(jnp.int32, (prefix_rows, comp_rows), 0)
    prefix_bias = jnp.where(prefix_id < plen_ref[0], 0.0, NEG).astype(BF16)
    for r in range(rollouts):
        keys[r, pl.ds(0, prefix_rows), pl.ds(DH, comp_rows)] = prefix_bias
        keys[r, pl.ds(prefix_rows, comp_rows), pl.ds(DH, comp_rows)] = causal
    position = lax.rem(
        lax.broadcasted_iota(jnp.int32, (1, tile_rows), 1), jnp.int32(comp_rows)
    )

    for kv in range(kv_local):
        for r in range(rollouts):
            lanes = pl.ds(kv * DH, DH)
            key_one = kvc_ref[0, 0, r, :, lanes]
            value_one = kvc_ref[1, 0, r, :, lanes]
            keys[r, pl.ds(prefix_rows, comp_rows), pl.ds(0, DH)] = key_one
            values[r, pl.ds(prefix_rows, comp_rows), :] = value_one
            keys_t[r, :, pl.ds(prefix_rows, comp_rows)] = key_one.astype(F32).T.astype(BF16)
            values_t[r, :, pl.ds(prefix_rows, comp_rows)] = value_one.astype(F32).T.astype(BF16)
        for j in range(1, peers):
            gather_copy(kv, j, ahead(j), behind(j)).wait_recv()
        key_prefix = landed[kv, 0]
        value_prefix = landed[kv, 1]
        key_prefix_t = key_prefix.astype(F32).T.astype(BF16)
        value_prefix_t = value_prefix.astype(F32).T.astype(BF16)
        for r in range(rollouts):
            keys[r, pl.ds(0, prefix_rows), pl.ds(0, DH)] = key_prefix
            values[r, pl.ds(0, prefix_rows), :] = value_prefix
            keys_t[r, :, pl.ds(0, prefix_rows)] = key_prefix_t
            values_t[r, :, pl.ds(0, prefix_rows)] = value_prefix_t
        acc_k[...] = jnp.zeros_like(acc_k)
        acc_v[...] = jnp.zeros_like(acc_v)

        def tile_step(i, carry, kv=kv):
            r = lax.div(i, tiles)
            first = kv * repeats + lax.rem(i, tiles) * HEADS_TILE
            lane_of = [
                pl.ds(pl.multiple_of((first + n) * DH, DH), DH) for n in range(HEADS_TILE)
            ]
            queries = [q_ref[0, r, :, lane] for lane in lane_of]
            grads = [g_ref[0, r, :, lane] for lane in lane_of]
            query = jnp.concatenate(queries, axis=0)
            grad = jnp.concatenate(grads, axis=0)
            query_bias = jnp.concatenate([query, jnp.concatenate([one_hot] * HEADS_TILE, axis=0)], axis=1)
            scores = dot(keys[r], query_bias, ((1,), (1,)))
            row_max = jnp.max(scores, axis=0, keepdims=True)
            exps = jnp.exp2((scores - row_max) * EXP2_SCALE)
            total = jnp.sum(exps, axis=0, keepdims=True)
            inverse = jnp.where(position < clen_ref[0, r], 1.0 / total, 0.0)
            weights32 = exps * inverse
            weights = weights32.astype(BF16)
            attended_t = dot(values_t[r], weights, ((1,), (0,))).astype(BF16).astype(F32)
            grad_t = grad.astype(F32).T
            delta = jnp.sum(attended_t * grad_t, axis=0, keepdims=True)
            slopes = dot(values[r], grad, ((1,), (1,)))
            ds = (weights32 * (slopes - delta)).astype(BF16)
            grad_query = (dot(keys_t[r], ds, ((1,), (0,))) * SCALE).T.astype(BF16)
            attended = attended_t.T.astype(BF16)
            for n in range(HEADS_TILE):
                rows = slice(n * comp_rows, (n + 1) * comp_rows)
                att_ref[0, r, :, lane_of[n]] = attended[rows]
                dq_ref[0, r, :, lane_of[n]] = grad_query[rows]
            acc_v[r] += dot(weights, grad, ((1,), (0,)))
            acc_k[r] += dot(ds, query, ((1,), (0,)))
            return carry

        lax.fori_loop(0, rollouts * tiles, tile_step, 0)

        for r in range(rollouts):
            comp = pl.ds(prefix_rows, comp_rows)
            gc_ref[0, 0, r, :, pl.ds(kv * DH, DH)] = (acc_k[r, comp, :] * SCALE).astype(BF16)
            gc_ref[1, 0, r, :, pl.ds(kv * DH, DH)] = acc_v[r, comp, :].astype(BF16)
        prefix = pl.ds(0, prefix_rows)
        key_total = acc_k[0, prefix, :]
        value_total = acc_v[0, prefix, :]
        for r in range(1, rollouts):
            key_total += acc_k[r, prefix, :]
            value_total += acc_v[r, prefix, :]
        outgoing[kv, 0] = (key_total * SCALE).astype(BF16)
        outgoing[kv, 1] = value_total.astype(BF16)
        for j in range(1, peers):
            reduce_copy(kv, j, ahead(j), me).start()
        incoming[kv, me] = outgoing[kv, :, rows_of(me), :]

    for kv in range(kv_local):
        for j in range(1, peers):
            reduce_copy(kv, j, ahead(j), behind(j)).wait_recv()
        for h in range(heads):
            for kind in range(2):
                sum32 = incoming[kv, h, kind].astype(F32)
                for s in range(1, samples):
                    sum32 += incoming[kv, s * heads + h, kind].astype(F32)
                gp_ref[kind, 0, :, pl.ds((h * kv_local + kv) * DH, DH)] = sum32.astype(BF16)
    for kv in range(kv_local):
        for j in range(1, peers):
            gather_copy(kv, j, ahead(j), me).wait_send()
            reduce_copy(kv, j, ahead(j), me).wait_send()


def body(queries, kv_comp, kv_prefix, grad_out, prompt_len, comp_len):
    samples = lax.axis_size("sample")
    heads = lax.axis_size("head")
    peers = samples * heads
    kv_local = kv_comp.shape[4] // DH
    rollouts, comp_rows = queries.shape[1], queries.shape[2]
    block_rows = kv_prefix.shape[2]
    prefix_rows = block_rows * peers
    all_rows = prefix_rows + comp_rows
    vmem = pl.BlockSpec(memory_space=pltpu.VMEM)
    smem = pl.BlockSpec(memory_space=pltpu.SMEM)
    return pl.pallas_call(
        functools.partial(kernel, samples, heads),
        out_shape=(
            jax.ShapeDtypeStruct(queries.shape, BF16),
            jax.ShapeDtypeStruct(queries.shape, BF16),
            jax.ShapeDtypeStruct(kv_comp.shape, BF16),
            jax.ShapeDtypeStruct(kv_prefix.shape, BF16),
        ),
        in_specs=[smem, smem, vmem, vmem, vmem, vmem],
        out_specs=(vmem, vmem, vmem, vmem),
        scratch_shapes=[
            pltpu.VMEM((kv_local, 2, prefix_rows, DH), BF16),
            pltpu.VMEM((rollouts, all_rows, DH + comp_rows), BF16),
            pltpu.VMEM((rollouts, all_rows, DH), BF16),
            pltpu.VMEM((rollouts, DH, all_rows), BF16),
            pltpu.VMEM((rollouts, DH, all_rows), BF16),
            pltpu.VMEM((rollouts, all_rows, DH), F32),
            pltpu.VMEM((rollouts, all_rows, DH), F32),
            pltpu.VMEM((kv_local, 2, prefix_rows, DH), BF16),
            pltpu.VMEM((kv_local, peers, 2, block_rows, DH), BF16),
            pltpu.SemaphoreType.DMA((kv_local, peers)),
            pltpu.SemaphoreType.DMA((kv_local, peers)),
            pltpu.SemaphoreType.DMA((kv_local, peers)),
            pltpu.SemaphoreType.DMA((kv_local, peers)),
        ],
        compiler_params=pltpu.CompilerParams(
            collective_id=0, has_side_effects=True, vmem_limit_bytes=56 * 1024 * 1024
        ),
    )(prompt_len, comp_len, queries, grad_out, kv_comp, kv_prefix)


def solution(mesh):
    return jax.shard_map(
        body,
        mesh=mesh,
        in_specs=(
            P("group", "sample", None, "head"),
            P(None, "group", "sample", None, "head"),
            P(None, "group", ("sample", "head"), None),
            P("group", "sample", None, "head"),
            P("group"),
            P("group", "sample"),
        ),
        out_specs=(
            P("group", "sample", None, "head"),
            P("group", "sample", None, "head"),
            P(None, "group", "sample", None, "head"),
            P(None, "group", ("sample", "head"), None),
        ),
        check_vma=False,
    )
```

time: 124 us -> 53.3 us (0.43)
  Pallas kernels: 0 us -> 46.5 us
  blocking collectives: 35.9 us -> 0 us
  matrix products: 29.1 us -> 0 us
  local copies, waits for them, and re-layouts: 23.6 us -> 5.23 us
  waiting for transfers between devices: 13.9 us -> 0 us
  starting transfers between devices: 11.1 us -> 0 us
  other arithmetic: 7.54 us -> 0 us
  between operations: 2.66 us -> 1.3 us
    pallas_call x0 -> x1, Pallas kernels: none -> 46.5 us  [body(): pl.pallas_call(functools.partial(kernel, samples, heads), out_shape=(jax....]
    dot_general x24 -> x0, matrix products: 29.1 us -> none  [the longest x2 5.93 us: body(): jnp.einsum('rjtp,pd->rtjd', weights_prefix, value_prefix_one, preferred_e...]
    unnamed x1 -> x0, blocking collectives: 27.4 us -> none
    all_to_all x2 -> x0, waiting for transfers between devices: 13.9 us -> none  [the longest x1 13.9 us: body(): lax.all_to_all(reordered, 'head', split_axis=0, concat_axis=2, tiled=True)]
    all_to_all x2 -> x0, starting transfers between devices: 11.1 us -> none  [the longest x1 6.32 us: body(): lax.all_to_all(kv_prefix, 'head', split_axis=3, concat_axis=2, tiled=True)]
    all_gather x1 -> x0, blocking collectives: 8.44 us -> none  [body(): own_prefix = lax.all_gather(regrouped, 'sample', axis=2, tiled=True)]
    unnamed x82 -> x10, local copies, waits for them, and re-layouts: 12 us -> 5.23 us
    convert_element_type x2 -> x0, other arithmetic: 4.49 us -> none  [the longest x1 3.84 us: body(): weights_prefix = weights_prefix32.astype(jnp.bfloat16)]
  transfers between devices with their start and end apart: 2 -> 0, of which waited for: 1 -> 0; matrix products, arithmetic and copies ran while one was open for 16% -> 0% of each run, Pallas kernels for 0% -> 0%
where the time goes in v1:
time: 53.3 us; the launch traced here: 53 us
  Pallas kernels  46.5 us (87%)
  local copies, waits for them, and re-layouts  5.23 us (10%)
  between operations  1.3 us (2%)
    pallas_call x1, Pallas kernels, body(): pl.pallas_call(functools.partial(kernel, samples, heads), out_shape=(jax....  46.5 us
    unnamed x10, local copies, waits for them, and re-layouts  5.23 us

profile of v1, /device:TPU:0, one launch (start us, length us, event | category | flops | bytes accessed | tf_op | source)
XLA Modules:
  0.0 53.0 jit_solution(8065109986849039918)
XLA Ops:
  1.3 46.5 %shard_map.93 = (bf16[1,2,128,2048]{3,2,1,0:T(8,128)(2,1)}, bf16[1,2,128,2048]{3,2,1,0:T(8,128)(2,1)}, bf16[2,1,2,128,256]{4,3,2,1,0:T(8,128)(2,1)}, bf16[2,1,64,1024]{3,2,1,0:T(8,128)(2,1)}) custom-call(s32[1]{0:T(128)S(6)} %copy.14.plen_ref, s32[1,2]{1,0:T(1,128)} %clen_ref.1, bf16[1,2,128,2048]{3,2,1,0:T(8,128)(2,1)} %q_ref.1, ...), custom_call_target="tpu_custom_call" | custom-call | tf_op jit(solution)/shard_map/pallas_call | solution.py:222
  47.8 0.0 copy-start
  47.8 2.4 %copy.15 = bf16[1,2,128,2048]{3,2,1,0:T(8,128)(2,1)} copy(bf16[1,2,128,2048]{3,2,1,0:T(8,128)(2,1)} %get-tuple-element.8) | data formatting | bytes 2097152
  50.2 0.0 copy-done
  50.2 0.0 copy-start.2
  50.2 1.0 %copy.16 = bf16[1,2,128,2048]{3,2,1,0:T(8,128)(2,1)} copy(bf16[1,2,128,2048]{3,2,1,0:T(8,128)(2,1)S(1)} %copy-done) | data formatting | bytes 2097152
  51.2 0.1 copy-done.2
  51.3 0.0 copy-start.1
  51.3 0.7 %copy.17 = bf16[2,1,2,128,256]{4,3,2,1,0:T(8,128)(2,1)} copy(bf16[2,1,2,128,256]{4,3,2,1,0:T(8,128)(2,1)S(1)} %copy-done.2) | data formatting | bytes 524288
  52.0 0.3 copy-done.1
  52.3 0.7 %copy.18 = bf16[2,1,64,1024]{3,2,1,0:T(8,128)(2,1)} copy(bf16[2,1,64,1024]{3,2,1,0:T(8,128)(2,1)S(1)} %copy-done.1) | data formatting | bytes 524288
Async XLA Ops:
  47.8 2.4 %copy-start = (bf16[1,2,128,2048]{3,2,1,0:T(8,128)(2,1)S(1)}, bf16[1,2,128,2048]{3,2,1,0:T(8,128)(2,1)}, u32[]{:S(2)}) copy-start(bf16[1,2,128,2048]{3,2,1,0:T(8,128)(2,1)} %get-tuple-element.9) | copy-start | bytes 3145732
  50.2 1.1 %copy-start.2 = (bf16[2,1,2,128,256]{4,3,2,1,0:T(8,128)(2,1)S(1)}, bf16[2,1,2,128,256]{4,3,2,1,0:T(8,128)(2,1)}, u32[]{:S(2)}) copy-start(bf16[2,1,2,128,256]{4,3,2,1,0:T(8,128)(2,1)} %get-tuple-element.10) | copy-start | bytes 786436
  51.3 1.0 %copy-start.1 = (bf16[2,1,64,1024]{3,2,1,0:T(8,128)(2,1)S(1)}, bf16[2,1,64,1024]{3,2,1,0:T(8,128)(2,1)}, u32[]{:S(2)}) copy-start(bf16[2,1,64,1024]{3,2,1,0:T(8,128)(2,1)} %get-tuple-element.11) | copy-start | bytes 786436

commit v2 on v1

v2 whole, which is shorter than its diff:
```python
import functools

import jax
import jax.numpy as jnp
from jax import lax
from jax.experimental import pallas as pl
from jax.experimental.pallas import tpu as pltpu
from jax.sharding import PartitionSpec as P

DH = 128
NEG = -1e30
MESH = pl.DeviceIdType.MESH
SCALE = 1.0 / DH**0.5
EXP2_SCALE = SCALE * 1.4426950408889634
F32 = jnp.float32
BF16 = jnp.bfloat16


def heads_per_tile(prefix_rows):
    return 4 if prefix_rows <= 1024 else 2


def dot(a, b, dims):
    return lax.dot_general(a, b, (dims, ((), ())), preferred_element_type=F32)


def kernel(
    samples,
    heads,
    plen_ref,
    clen_ref,
    q_ref,
    g_ref,
    kvc_ref,
    kvp_ref,
    att_ref,
    dq_ref,
    gc_ref,
    gp_ref,
    landed,
    keys,
    values,
    keys_t,
    values_t,
    acc_k,
    acc_v,
    held,
    held_ds,
    outgoing,
    incoming,
    send_a,
    recv_a,
    send_b,
    recv_b,
):
    peers = samples * heads
    kv_local = kvc_ref.shape[4] // DH
    rollouts, comp_rows = q_ref.shape[1], q_ref.shape[2]
    repeats = q_ref.shape[3] // kvc_ref.shape[4]
    block_rows = kvp_ref.shape[2]
    prefix_rows = block_rows * peers
    all_rows = prefix_rows + comp_rows
    tile_heads = heads_per_tile(prefix_rows)
    tiles = repeats // tile_heads
    tile_rows = tile_heads * comp_rows
    me = lax.axis_index("sample") * heads + lax.axis_index("head")

    def device(block):
        return {"sample": lax.div(block, heads), "head": lax.rem(block, heads)}

    def ahead(j):
        return lax.rem(me + j, peers)

    def behind(j):
        return lax.rem(me + peers - j, peers)

    def rows_of(block):
        return pl.ds(pl.multiple_of(block * block_rows, block_rows), block_rows)

    def lanes_of(block, kv):
        head = lax.rem(block, heads)
        return pl.ds(pl.multiple_of((head * kv_local + kv) * DH, DH), DH)

    def gather_copy(kv, kind, j, to, owner):
        return pltpu.make_async_remote_copy(
            src_ref=kvp_ref.at[kind, 0, :, lanes_of(to, kv)],
            dst_ref=landed.at[kv, kind, rows_of(owner), :],
            send_sem=send_a.at[kv, kind, j],
            recv_sem=recv_a.at[kv, kind, j],
            device_id=device(to),
            device_id_type=MESH,
        )

    def reduce_copy(kv, kind, j, to, owner):
        return pltpu.make_async_remote_copy(
            src_ref=outgoing.at[kv, kind, rows_of(to), :],
            dst_ref=incoming.at[kv, kind, owner],
            send_sem=send_b.at[kv, kind, j],
            recv_sem=recv_b.at[kv, kind, j],
            device_id=device(to),
            device_id_type=MESH,
        )

    def send_prompt(kv, kind):
        for j in range(1, peers):
            gather_copy(kv, kind, j, ahead(j), me).start()

    def prompt_arrived(kv, kind):
        for j in range(1, peers):
            gather_copy(kv, kind, j, ahead(j), behind(j)).wait_recv()

    barrier = pltpu.get_barrier_semaphore()
    for j in range(1, peers):
        pl.semaphore_signal(barrier, inc=1, device_id=device(ahead(j)), device_id_type=MESH)

    row_id = lax.broadcasted_iota(jnp.int32, (comp_rows, comp_rows), 0)
    lane_id = lax.broadcasted_iota(jnp.int32, (comp_rows, comp_rows), 1)
    one_hot = jnp.where(row_id == lane_id, 1.0, 0.0).astype(BF16)
    causal = jnp.where(row_id <= lane_id, 0.0, NEG).astype(BF16)
    prefix_id = lax.broadcasted_iota(jnp.int32, (prefix_rows, comp_rows), 0)
    prefix_bias = jnp.where(prefix_id < plen_ref[0], 0.0, NEG).astype(BF16)
    prefix = pl.ds(0, prefix_rows)
    comp = pl.ds(prefix_rows, comp_rows)
    for r in range(rollouts):
        keys[r, prefix, pl.ds(DH, comp_rows)] = prefix_bias
        keys[r, comp, pl.ds(DH, comp_rows)] = causal
    for kv in range(kv_local):
        landed[kv, :, rows_of(me), :] = kvp_ref[:, 0, :, lanes_of(me, kv)]
    position = lax.rem(
        lax.broadcasted_iota(jnp.int32, (1, tile_rows), 1), jnp.int32(comp_rows)
    )

    pl.semaphore_wait(barrier, peers - 1)
    send_prompt(0, 0)
    send_prompt(0, 1)

    def tile_place(i, kv):
        r = lax.div(i, tiles)
        first = kv * repeats + lax.rem(i, tiles) * tile_heads
        return r, [pl.ds(pl.multiple_of((first + n) * DH, DH), DH) for n in range(tile_heads)]

    def stacked(ref, r, lanes):
        return jnp.concatenate([ref[0, r, :, lane] for lane in lanes], axis=0)

    def each_tile(step):
        lax.fori_loop(0, rollouts * tiles, step, 0)

    def finish(kv, kind, acc, factor):
        mine = pl.ds(kv * DH, DH)
        total = acc[0, prefix, :]
        for r in range(1, rollouts):
            total += acc[r, prefix, :]
        outgoing[kv, kind] = (total * factor).astype(BF16)
        for j in range(1, peers):
            reduce_copy(kv, kind, j, ahead(j), me).start()
        incoming[kv, kind, me] = outgoing[kv, kind, rows_of(me), :]
        for r in range(rollouts):
            gc_ref[kind, 0, r, :, mine] = (acc[r, comp, :] * factor).astype(BF16)

    for kv in range(kv_local):
        mine = pl.ds(kv * DH, DH)
        for r in range(rollouts):
            key_one = kvc_ref[0, 0, r, :, mine]
            value_one = kvc_ref[1, 0, r, :, mine]
            keys[r, comp, pl.ds(0, DH)] = key_one
            values[r, comp, :] = value_one
            keys_t[r, :, comp] = key_one.astype(F32).T.astype(BF16)
            values_t[r, :, comp] = value_one.astype(F32).T.astype(BF16)
        acc_k[...] = jnp.zeros_like(acc_k)
        acc_v[...] = jnp.zeros_like(acc_v)

        prompt_arrived(kv, 0)
        if kv + 1 < kv_local:
            send_prompt(kv + 1, 0)
            send_prompt(kv + 1, 1)
        key_prefix = landed[kv, 0]
        key_prefix_t = key_prefix.astype(F32).T.astype(BF16)
        for r in range(rollouts):
            keys[r, prefix, pl.ds(0, DH)] = key_prefix
            keys_t[r, :, prefix] = key_prefix_t

        def weigh(i, carry, kv=kv):
            r, lanes = tile_place(i, kv)
            query_bias = jnp.concatenate(
                [stacked(q_ref, r, lanes), jnp.concatenate([one_hot] * tile_heads, axis=0)], axis=1
            )
            scores = dot(keys[r], query_bias, ((1,), (1,)))
            row_max = jnp.max(scores, axis=0, keepdims=True)
            exps = jnp.exp2((scores - row_max) * EXP2_SCALE)
            total = jnp.sum(exps, axis=0, keepdims=True)
            inverse = jnp.where(position < clen_ref[0, r], 1.0 / total, 0.0)
            weights32 = exps * inverse
            held[i] = weights32
            acc_v[r] += dot(weights32.astype(BF16), stacked(g_ref, r, lanes), ((1,), (0,)))
            return carry

        each_tile(weigh)
        finish(kv, 1, acc_v, 1.0)

        prompt_arrived(kv, 1)
        value_prefix = landed[kv, 1]
        value_prefix_t = value_prefix.astype(F32).T.astype(BF16)
        for r in range(rollouts):
            values[r, prefix, :] = value_prefix
            values_t[r, :, prefix] = value_prefix_t

        def slope(i, carry, kv=kv):
            r, lanes = tile_place(i, kv)
            grad = stacked(g_ref, r, lanes)
            weights32 = held[i]
            attended_t = dot(values_t[r], weights32.astype(BF16), ((1,), (0,))).astype(BF16).astype(F32)
            delta = jnp.sum(attended_t * grad.astype(F32).T, axis=0, keepdims=True)
            slopes = dot(values[r], grad, ((1,), (1,)))
            ds = (weights32 * (slopes - delta)).astype(BF16)
            held_ds[i] = ds
            attended = attended_t.T.astype(BF16)
            for n in range(tile_heads):
                att_ref[0, r, :, lanes[n]] = attended[n * comp_rows : (n + 1) * comp_rows]
            acc_k[r] += dot(ds, stacked(q_ref, r, lanes), ((1,), (0,)))
            return carry

        each_tile(slope)
        finish(kv, 0, acc_k, SCALE)

        def query_grad(i, carry, kv=kv):
            r, lanes = tile_place(i, kv)
            grad_query = (dot(keys_t[r], held_ds[i], ((1,), (0,))) * SCALE).T.astype(BF16)
            for n in range(tile_heads):
                dq_ref[0, r, :, lanes[n]] = grad_query[n * comp_rows : (n + 1) * comp_rows]
            return carry

        each_tile(query_grad)

    for kv in range(kv_local):
        for kind in (1, 0):
            for j in range(1, peers):
                reduce_copy(kv, kind, j, ahead(j), behind(j)).wait_recv()
            for h in range(heads):
                sum32 = incoming[kv, kind, h].astype(F32)
                for s in range(1, samples):
                    sum32 += incoming[kv, kind, s * heads + h].astype(F32)
                gp_ref[kind, 0, :, pl.ds((h * kv_local + kv) * DH, DH)] = sum32.astype(BF16)
    for kv in range(kv_local):
        for kind in range(2):
            for j in range(1, peers):
                gather_copy(kv, kind, j, ahead(j), me).wait_send()
                reduce_copy(kv, kind, j, ahead(j), me).wait_send()


def write_out(*refs):
    sources, targets, sems = refs[:4], refs[4:8], refs[8]
    copies = [pltpu.make_async_copy(sources[i], targets[i], sems.at[i]) for i in range(4)]
    for copy in copies:
        copy.start()
    for copy in copies:
        copy.wait()


def body(queries, kv_comp, kv_prefix, grad_out, prompt_len, comp_len):
    samples = lax.axis_size("sample")
    heads = lax.axis_size("head")
    peers = samples * heads
    kv_local = kv_comp.shape[4] // DH
    rollouts, comp_rows = queries.shape[1], queries.shape[2]
    block_rows = kv_prefix.shape[2]
    prefix_rows = block_rows * peers
    all_rows = prefix_rows + comp_rows
    tile_heads = heads_per_tile(prefix_rows)
    tile_count = queries.shape[3] // DH // kv_local // tile_heads * rollouts
    vmem = pl.BlockSpec(memory_space=pltpu.VMEM)
    smem = pl.BlockSpec(memory_space=pltpu.SMEM)
    shapes = (queries.shape, queries.shape, kv_comp.shape, kv_prefix.shape)
    results = pl.pallas_call(
        functools.partial(kernel, samples, heads),
        out_shape=tuple(pltpu.VMEM(shape, BF16) for shape in shapes),
        in_specs=[smem, smem, vmem, vmem, vmem, vmem],
        out_specs=(vmem, vmem, vmem, vmem),
        scratch_shapes=[
            pltpu.VMEM((kv_local, 2, prefix_rows, DH), BF16),
            pltpu.VMEM((rollouts, all_rows, DH + comp_rows), BF16),
            pltpu.VMEM((rollouts, all_rows, DH), BF16),
            pltpu.VMEM((rollouts, DH, all_rows), BF16),
            pltpu.VMEM((rollouts, DH, all_rows), BF16),
            pltpu.VMEM((rollouts, all_rows, DH), F32),
            pltpu.VMEM((rollouts, all_rows, DH), F32),
            pltpu.VMEM((tile_count, all_rows, tile_heads * comp_rows), F32),
            pltpu.VMEM((tile_count, all_rows, tile_heads * comp_rows), BF16),
            pltpu.VMEM((kv_local, 2, prefix_rows, DH), BF16),
            pltpu.VMEM((kv_local, 2, peers, block_rows, DH), BF16),
            pltpu.SemaphoreType.DMA((kv_local, 2, peers)),
            pltpu.SemaphoreType.DMA((kv_local, 2, peers)),
            pltpu.SemaphoreType.DMA((kv_local, 2, peers)),
            pltpu.SemaphoreType.DMA((kv_local, 2, peers)),
        ],
        compiler_params=pltpu.CompilerParams(
            collective_id=0, has_side_effects=True, vmem_limit_bytes=60 * 1024 * 1024
        ),
    )(prompt_len, comp_len, queries, grad_out, kv_comp, kv_prefix)
    return pl.pallas_call(
        write_out,
        out_shape=tuple(jax.ShapeDtypeStruct(shape, BF16) for shape in shapes),
        in_specs=[vmem] * 4,
        out_specs=(pl.BlockSpec(memory_space=pl.ANY),) * 4,
        scratch_shapes=[pltpu.SemaphoreType.DMA((4,))],
    )(*results)


def solution(mesh):
    return jax.shard_map(
        body,
        mesh=mesh,
        in_specs=(
            P("group", "sample", None, "head"),
            P(None, "group", "sample", None, "head"),
            P(None, "group", ("sample", "head"), None),
            P("group", "sample", None, "head"),
            P("group"),
            P("group", "sample"),
        ),
        out_specs=(
            P("group", "sample", None, "head"),
            P("group", "sample", None, "head"),
            P(None, "group", "sample", None, "head"),
            P(None, "group", ("sample", "head"), None),
        ),
        check_vma=False,
    )
```

time: 53.3 us -> 43.1 us (0.81)
  Pallas kernels: 46.5 us -> 38.3 us
  local copies, waits for them, and re-layouts: 5.23 us -> 3.37 us
    pallas_call x1 -> x2, Pallas kernels: 46.5 us -> 38.3 us  [the longest x1 35.1 us: body(): pl.pallas_call(functools.partial(kernel, samples, heads), out_shape=tuple...]
    unnamed x10 -> x8, local copies, waits for them, and re-layouts: 5.23 us -> 3.37 us
where the time goes in v2:
time: 43.1 us; the launch traced here: 42.9 us
  Pallas kernels  38.3 us (89%)
  local copies, waits for them, and re-layouts  3.37 us (8%)
  between operations  1.3 us (3%)
    pallas_call x1, Pallas kernels, body(): pl.pallas_call(functools.partial(kernel, samples, heads), out_shape=tuple...  35.1 us
    unnamed x8, local copies, waits for them, and re-layouts  3.37 us
    pallas_call x1, Pallas kernels, body(): pl.pallas_call(write_out, out_shape=tuple((jax.ShapeDtypeStruct(shape, BF...  3.17 us

profile of v2, /device:TPU:0, one launch (start us, length us, event | category | flops | bytes accessed | tf_op | source)
XLA Modules:
  0.0 42.9 jit_solution(12414503433342640432)
XLA Ops:
  1.3 35.1 %shard_map.93 = (bf16[1,2,128,2048]{3,2,1,0:T(8,128)(2,1)S(1)}, bf16[1,2,128,2048]{3,2,1,0:T(8,128)(2,1)S(1)}, bf16[2,1,2,128,256]{4,3,2,1,0:T(8,128)(2,1)S(1)}, bf16[2,1,64,1024]{3,2,1,0:T(8,128)(2,1)S(1)}) custom-call(s32[1]{0:T(128)S(6)} %copy.10.plen_ref, s32[1,2]{1,0:T(1,128)} %clen_ref.1, bf16[1,2,128,2048]{3,2,1,0:T(8,128)(2,1)} %q_ref.1, ...), custom_call_target="tpu_custom_call" | custom-call | tf_op jit(solution)/shard_map/pallas_call | solution.py:273
  36.4 0.0 copy-start
  36.4 1.0 %copy-done = bf16[1,2,128,2048]{3,2,1,0:T(8,128)(2,1)} copy-done((bf16[1,2,128,2048]{3,2,1,0:T(8,128)(2,1)}, bf16[1,2,128,2048]{3,2,1,0:T(8,128)(2,1)S(1)}, u32[]{:S(2)}) %copy-start) | copy-done | bytes 1048600
  37.3 0.0 copy-start.1
  37.3 1.0 %copy-done.1 = bf16[1,2,128,2048]{3,2,1,0:T(8,128)(2,1)} copy-done((bf16[1,2,128,2048]{3,2,1,0:T(8,128)(2,1)}, bf16[1,2,128,2048]{3,2,1,0:T(8,128)(2,1)S(1)}, u32[]{:S(2)}) %copy-start.1) | copy-done | bytes 1048600
  38.3 0.0 copy-start.2
  38.4 0.7 %copy-done.2 = bf16[2,1,2,128,256]{4,3,2,1,0:T(8,128)(2,1)} copy-done((bf16[2,1,2,128,256]{4,3,2,1,0:T(8,128)(2,1)}, bf16[2,1,2,128,256]{4,3,2,1,0:T(8,128)(2,1)S(1)}, u32[]{:S(2)}) %copy-start.2) | copy-done | bytes 262168
  39.1 0.0 copy-start.3
  39.1 0.7 %copy-done.3 = bf16[2,1,64,1024]{3,2,1,0:T(8,128)(2,1)} copy-done((bf16[2,1,64,1024]{3,2,1,0:T(8,128)(2,1)}, bf16[2,1,64,1024]{3,2,1,0:T(8,128)(2,1)S(1)}, u32[]{:S(2)}) %copy-start.3) | copy-done | bytes 262168
  39.8 3.2 %shard_map.94 = (bf16[1,2,128,2048]{3,2,1,0:T(8,128)(2,1)}, bf16[1,2,128,2048]{3,2,1,0:T(8,128)(2,1)}, bf16[2,1,2,128,256]{4,3,2,1,0:T(8,128)(2,1)}, bf16[2,1,64,1024]{3,2,1,0:T(8,128)(2,1)}) custom-call(bf16[1,2,128,2048]{3,2,1,0:T(8,128)(2,1)} %copy-done, bf16[1,2,128,2048]{3,2,1,0:T(8,128)(2,1)} %copy-done.1, bf16[2,1,2,128,256]{4,3,2,1,0:T(8,128)(2,1)} %copy-done.2, ...), custom_call_target="tpu_custom_call" | custom-call | tf_op jit(solution)/shard_map/pallas_call | solution.py:299
Async XLA Ops:
  36.4 1.0 %copy-start = (bf16[1,2,128,2048]{3,2,1,0:T(8,128)(2,1)}, bf16[1,2,128,2048]{3,2,1,0:T(8,128)(2,1)S(1)}, u32[]{:S(2)}) copy-start(bf16[1,2,128,2048]{3,2,1,0:T(8,128)(2,1)S(1)} %get-tuple-element.8.refs_0_) | copy-start | bytes 3145732
  37.3 1.0 %copy-start.1 = (bf16[1,2,128,2048]{3,2,1,0:T(8,128)(2,1)}, bf16[1,2,128,2048]{3,2,1,0:T(8,128)(2,1)S(1)}, u32[]{:S(2)}) copy-start(bf16[1,2,128,2048]{3,2,1,0:T(8,128)(2,1)S(1)} %get-tuple-element.9.refs_1_) | copy-start | bytes 3145732
  38.3 0.7 %copy-start.2 = (bf16[2,1,2,128,256]{4,3,2,1,0:T(8,128)(2,1)}, bf16[2,1,2,128,256]{4,3,2,1,0:T(8,128)(2,1)S(1)}, u32[]{:S(2)}) copy-start(bf16[2,1,2,128,256]{4,3,2,1,0:T(8,128)(2,1)S(1)} %get-tuple-element.10.refs_2_) | copy-start | bytes 786436
  39.1 0.7 %copy-start.3 = (bf16[2,1,64,1024]{3,2,1,0:T(8,128)(2,1)}, bf16[2,1,64,1024]{3,2,1,0:T(8,128)(2,1)S(1)}, u32[]{:S(2)}) copy-start(bf16[2,1,64,1024]{3,2,1,0:T(8,128)(2,1)S(1)} %get-tuple-element.11.refs_3_) | copy-start | bytes 786436

commit v3 on v2

--- a/solution.py
+++ b/solution.py
@@ -17,7 +17,7 @@
 
 
 def heads_per_tile(prefix_rows):
-    return 4 if prefix_rows <= 1024 else 2
+    return 8 if prefix_rows <= 1024 else 2
 
 
 def dot(a, b, dims):
@@ -143,7 +143,7 @@
         return jnp.concatenate([ref[0, r, :, lane] for lane in lanes], axis=0)
 
     def each_tile(step):
-        lax.fori_loop(0, rollouts * tiles, step, 0)
+        lax.fori_loop(0, rollouts * tiles, step, 0, unroll=2)
 
     def finish(kv, kind, acc, factor):
         mine = pl.ds(kv * DH, DH)
@@ -299,9 +299,10 @@
     return pl.pallas_call(
         write_out,
         out_shape=tuple(jax.ShapeDtypeStruct(shape, BF16) for shape in shapes),
-        in_specs=[vmem] * 4,
+        in_specs=[pl.BlockSpec(memory_space=pl.ANY)] * 4,
         out_specs=(pl.BlockSpec(memory_space=pl.ANY),) * 4,
         scratch_shapes=[pltpu.SemaphoreType.DMA((4,))],
+        compiler_params=pltpu.CompilerParams(vmem_limit_bytes=1024 * 1024),
     )(*results)
 
 

time: 43.1 us -> 35.6 us (0.83)
  Pallas kernels: 38.3 us -> 34.1 us
  local copies, waits for them, and re-layouts: 3.37 us -> 0 us
    unnamed x8 -> x0, local copies, waits for them, and re-layouts: 3.37 us -> none
    pallas_call x1, Pallas kernels: 35.1 us -> 32.6 us  [body(): pl.pallas_call(functools.partial(kernel, samples, heads), out_shape=tuple...]
    pallas_call x1, Pallas kernels: 3.17 us -> 1.52 us  [body(): pl.pallas_call(write_out, out_shape=tuple((jax.ShapeDtypeStruct(shape, BF...]
where the time goes in v3:
time: 35.6 us; the launch traced here: 35.4 us
  Pallas kernels  34.1 us (96%)
  between operations  1.29 us (4%)
    pallas_call x1, Pallas kernels, body(): pl.pallas_call(functools.partial(kernel, samples, heads), out_shape=tuple...  32.6 us
    pallas_call x1, Pallas kernels, body(): pl.pallas_call(write_out, out_shape=tuple((jax.ShapeDtypeStruct(shape, BF...  1.52 us

profile of v3, /device:TPU:0, one launch (start us, length us, event | category | flops | bytes accessed | tf_op | source)
XLA Modules:
  0.0 35.4 jit_solution(9886148652718849019)
XLA Ops:
  1.3 32.6 %shard_map.93 = (bf16[1,2,128,2048]{3,2,1,0:T(8,128)(2,1)S(1)}, bf16[1,2,128,2048]{3,2,1,0:T(8,128)(2,1)S(1)}, bf16[2,1,2,128,256]{4,3,2,1,0:T(8,128)(2,1)S(1)}, bf16[2,1,64,1024]{3,2,1,0:T(8,128)(2,1)S(1)}) custom-call(s32[1]{0:T(128)S(6)} %copy.10.plen_ref, s32[1,2]{1,0:T(1,128)} %clen_ref.1, bf16[1,2,128,2048]{3,2,1,0:T(8,128)(2,1)} %q_ref.1, ...), custom_call_target="tpu_custom_call" | custom-call | tf_op jit(solution)/shard_map/pallas_call | solution.py:273
  33.9 1.5 %shard_map.94 = (bf16[1,2,128,2048]{3,2,1,0:T(8,128)(2,1)}, bf16[1,2,128,2048]{3,2,1,0:T(8,128)(2,1)}, bf16[2,1,2,128,256]{4,3,2,1,0:T(8,128)(2,1)}, bf16[2,1,64,1024]{3,2,1,0:T(8,128)(2,1)}) custom-call(bf16[1,2,128,2048]{3,2,1,0:T(8,128)(2,1)S(1)} %get-tuple-element.8.refs_0_, bf16[1,2,128,2048]{3,2,1,0:T(8,128)(2,1)S(1)} %get-tuple-element.9.refs_1_, ...), custom_call_target="tpu_custom_call" | custom-call | tf_op jit(solution)/shard_map/pallas_call | solution.py:299

commit v4 on v3

--- a/solution.py
+++ b/solution.py
@@ -29,8 +29,8 @@
     heads,
     plen_ref,
     clen_ref,
-    q_ref,
-    g_ref,
+    q_any,
+    g_any,
     kvc_ref,
     kvp_ref,
     att_ref,
@@ -47,11 +47,22 @@
     held,
     held_ds,
     outgoing,
+    own,
     incoming,
+    summed,
+    final,
+    last,
+    q_ref,
+    g_ref,
+    load_sem,
     send_a,
     recv_a,
     send_b,
     recv_b,
+    send_c,
+    recv_c,
+    send_d,
+    recv_d,
 ):
     peers = samples * heads
     kv_local = kvc_ref.shape[4] // DH
@@ -63,7 +74,24 @@
     tile_heads = heads_per_tile(prefix_rows)
     tiles = repeats // tile_heads
     tile_rows = tile_heads * comp_rows
-    me = lax.axis_index("sample") * heads + lax.axis_index("head")
+    span = block_rows * heads
+    my_sample, my_head = lax.axis_index("sample"), lax.axis_index("head")
+    me = my_sample * heads + my_head
+
+    def other_head(j):
+        return lax.rem(my_head + j + heads, heads)
+
+    def other_sample(j):
+        return lax.rem(my_sample + j + samples, samples)
+
+    def rows_of(block):
+        return pl.ds(pl.multiple_of(block * block_rows, block_rows), block_rows)
+
+    def span_of(sample):
+        return pl.ds(pl.multiple_of(sample * span, span), span)
+
+    def lanes_of(head, kv):
+        return pl.ds(pl.multiple_of((head * kv_local + kv) * DH, DH), DH)
 
     def device(block):
         return {"sample": lax.div(block, heads), "head": lax.rem(block, heads)}
@@ -74,16 +102,10 @@
     def behind(j):
         return lax.rem(me + peers - j, peers)
 
-    def rows_of(block):
-        return pl.ds(pl.multiple_of(block * block_rows, block_rows), block_rows)
-
-    def lanes_of(block, kv):
-        head = lax.rem(block, heads)
-        return pl.ds(pl.multiple_of((head * kv_local + kv) * DH, DH), DH)
-
-    def gather_copy(kv, kind, j, to, owner):
+    def gather_copy(kv, kind, j, owner):
+        to = ahead(j)
         return pltpu.make_async_remote_copy(
-            src_ref=kvp_ref.at[kind, 0, :, lanes_of(to, kv)],
+            src_ref=kvp_ref.at[kind, 0, :, lanes_of(lax.rem(to, heads), kv)],
             dst_ref=landed.at[kv, kind, rows_of(owner), :],
             send_sem=send_a.at[kv, kind, j],
             recv_sem=recv_a.at[kv, kind, j],
@@ -91,24 +113,74 @@
             device_id_type=MESH,
         )
 
-    def reduce_copy(kv, kind, j, to, owner):
+    def reduce_copy(j, owner):
+        to = ahead(j)
         return pltpu.make_async_remote_copy(
-            src_ref=outgoing.at[kv, kind, rows_of(to), :],
-            dst_ref=incoming.at[kv, kind, owner],
-            send_sem=send_b.at[kv, kind, j],
-            recv_sem=recv_b.at[kv, kind, j],
+            src_ref=outgoing.at[kv_local - 1, 0, rows_of(to), :],
+            dst_ref=last.at[owner],
+            send_sem=send_b.at[j],
+            recv_sem=recv_b.at[j],
             device_id=device(to),
             device_id_type=MESH,
         )
 
+    def reduce_sample(kv, kind, j):
+        return pltpu.make_async_remote_copy(
+            src_ref=outgoing.at[kv, kind, span_of(other_sample(j)), :],
+            dst_ref=incoming.at[kv, kind, j],
+            send_sem=send_c.at[kv, kind, j],
+            recv_sem=recv_c.at[kv, kind, j],
+            device_id={"sample": other_sample(j)},
+            device_id_type=MESH,
+        )
+
+    def reduce_head(kv, kind, j):
+        return pltpu.make_async_remote_copy(
+            src_ref=summed.at[kv, kind, pl.ds(pl.multiple_of(other_head(j) * block_rows, block_rows), block_rows), :],
+            dst_ref=final.at[kv, kind, my_head],
+            send_sem=send_d.at[kv, kind, j],
+            recv_sem=recv_d.at[kv, kind, j],
+            device_id={"head": other_head(j)},
+            device_id_type=MESH,
+        )
+
+    def landing_final(kv, kind, j):
+        place = final.at[kv, kind, other_head(-j)]
+        return pltpu.make_async_remote_copy(
+            src_ref=place,
+            dst_ref=place,
+            send_sem=send_d.at[kv, kind, j],
+            recv_sem=recv_d.at[kv, kind, j],
+            device_id={"head": other_head(j)},
+            device_id_type=MESH,
+        )
+
     def send_prompt(kv, kind):
         for j in range(1, peers):
-            gather_copy(kv, kind, j, ahead(j), me).start()
+            gather_copy(kv, kind, j, me).start()
 
     def prompt_arrived(kv, kind):
         for j in range(1, peers):
-            gather_copy(kv, kind, j, ahead(j), behind(j)).wait_recv()
-
+            gather_copy(kv, kind, j, behind(j)).wait_recv()
+
+    def pass_gradient(kv, kind):
+        sum32 = own[kv, kind]
+        for j in range(1, samples):
+            reduce_sample(kv, kind, j).wait_recv()
+        for j in range(1, samples):
+            sum32 += incoming[kv, kind, j].astype(F32)
+        summed[kv, kind] = sum32.astype(BF16)
+        for j in range(1, heads):
+            reduce_head(kv, kind, j).start()
+        mine = pl.ds(pl.multiple_of(my_head * block_rows, block_rows), block_rows)
+        final[kv, kind, my_head] = summed[kv, kind, mine, :]
+
+    loads = [
+        pltpu.make_async_copy(q_any, q_ref, load_sem.at[0]),
+        pltpu.make_async_copy(g_any, g_ref, load_sem.at[1]),
+    ]
+    for load in loads:
+        load.start()
     barrier = pltpu.get_barrier_semaphore()
     for j in range(1, peers):
         pl.semaphore_signal(barrier, inc=1, device_id=device(ahead(j)), device_id_type=MESH)
@@ -125,7 +197,7 @@
         keys[r, prefix, pl.ds(DH, comp_rows)] = prefix_bias
         keys[r, comp, pl.ds(DH, comp_rows)] = causal
     for kv in range(kv_local):
-        landed[kv, :, rows_of(me), :] = kvp_ref[:, 0, :, lanes_of(me, kv)]
+        landed[kv, :, rows_of(me), :] = kvp_ref[:, 0, :, lanes_of(my_head, kv)]
     position = lax.rem(
         lax.broadcasted_iota(jnp.int32, (1, tile_rows), 1), jnp.int32(comp_rows)
     )
@@ -133,6 +205,8 @@
     pl.semaphore_wait(barrier, peers - 1)
     send_prompt(0, 0)
     send_prompt(0, 1)
+    for load in loads:
+        load.wait()
 
     def tile_place(i, kv):
         r = lax.div(i, tiles)
@@ -151,9 +225,18 @@
         for r in range(1, rollouts):
             total += acc[r, prefix, :]
         outgoing[kv, kind] = (total * factor).astype(BF16)
-        for j in range(1, peers):
-            reduce_copy(kv, kind, j, ahead(j), me).start()
-        incoming[kv, kind, me] = outgoing[kv, kind, rows_of(me), :]
+        if (kv, kind) == (kv_local - 1, 0):
+            for j in range(1, peers):
+                reduce_copy(j, me).start()
+            last[me] = outgoing[kv, kind, rows_of(me), :]
+        else:
+            for j in range(1, samples):
+                reduce_sample(kv, kind, j).start()
+            rows = span_of(my_sample)
+            own32 = acc[0, rows, :]
+            for r in range(1, rollouts):
+                own32 += acc[r, rows, :]
+            own[kv, kind] = own32 * factor
         for r in range(rollouts):
             gc_ref[kind, 0, r, :, mine] = (acc[r, comp, :] * factor).astype(BF16)
 
@@ -196,6 +279,8 @@
 
         each_tile(weigh)
         finish(kv, 1, acc_v, 1.0)
+        if kv > 0:
+            pass_gradient(kv - 1, 0)
 
         prompt_arrived(kv, 1)
         value_prefix = landed[kv, 1]
@@ -221,6 +306,7 @@
 
         each_tile(slope)
         finish(kv, 0, acc_k, SCALE)
+        pass_gradient(kv, 1)
 
         def query_grad(i, carry, kv=kv):
             r, lanes = tile_place(i, kv)
@@ -231,20 +317,30 @@
 
         each_tile(query_grad)
 
-    for kv in range(kv_local):
-        for kind in (1, 0):
-            for j in range(1, peers):
-                reduce_copy(kv, kind, j, ahead(j), behind(j)).wait_recv()
-            for h in range(heads):
-                sum32 = incoming[kv, kind, h].astype(F32)
-                for s in range(1, samples):
-                    sum32 += incoming[kv, kind, s * heads + h].astype(F32)
-                gp_ref[kind, 0, :, pl.ds((h * kv_local + kv) * DH, DH)] = sum32.astype(BF16)
+    two_step = [(kv, kind) for kv in range(kv_local) for kind in (1, 0)][:-1]
+    for kv, kind in two_step:
+        for j in range(1, heads):
+            landing_final(kv, kind, j).wait_recv()
+        for h in range(heads):
+            gp_ref[kind, 0, :, pl.ds((h * kv_local + kv) * DH, DH)] = final[kv, kind, h]
+    for j in range(1, peers):
+        reduce_copy(j, behind(j)).wait_recv()
+    for h in range(heads):
+        sum32 = last[h].astype(F32)
+        for s in range(1, samples):
+            sum32 += last[s * heads + h].astype(F32)
+        gp_ref[0, 0, :, pl.ds((h * kv_local + kv_local - 1) * DH, DH)] = sum32.astype(BF16)
     for kv in range(kv_local):
         for kind in range(2):
             for j in range(1, peers):
-                gather_copy(kv, kind, j, ahead(j), me).wait_send()
-                reduce_copy(kv, kind, j, ahead(j), me).wait_send()
+                gather_copy(kv, kind, j, me).wait_send()
+    for kv, kind in two_step:
+        for j in range(1, heads):
+            reduce_head(kv, kind, j).wait_send()
+        for j in range(1, samples):
+            reduce_sample(kv, kind, j).wait_send()
+    for j in range(1, peers):
+        reduce_copy(j, me).wait_send()
 
 
 def write_out(*refs):
@@ -268,12 +364,13 @@
     tile_heads = heads_per_tile(prefix_rows)
     tile_count = queries.shape[3] // DH // kv_local // tile_heads * rollouts
     vmem = pl.BlockSpec(memory_space=pltpu.VMEM)
+    hbm = pl.BlockSpec(memory_space=pl.ANY)
     smem = pl.BlockSpec(memory_space=pltpu.SMEM)
     shapes = (queries.shape, queries.shape, kv_comp.shape, kv_prefix.shape)
     results = pl.pallas_call(
         functools.partial(kernel, samples, heads),
         out_shape=tuple(pltpu.VMEM(shape, BF16) for shape in shapes),
-        in_specs=[smem, smem, vmem, vmem, vmem, vmem],
+        in_specs=[smem, smem, hbm, hbm, vmem, vmem],
         out_specs=(vmem, vmem, vmem, vmem),
         scratch_shapes=[
             pltpu.VMEM((kv_local, 2, prefix_rows, DH), BF16),
@@ -286,21 +383,32 @@
             pltpu.VMEM((tile_count, all_rows, tile_heads * comp_rows), F32),
             pltpu.VMEM((tile_count, all_rows, tile_heads * comp_rows), BF16),
             pltpu.VMEM((kv_local, 2, prefix_rows, DH), BF16),
-            pltpu.VMEM((kv_local, 2, peers, block_rows, DH), BF16),
+            pltpu.VMEM((kv_local, 2, block_rows * heads, DH), F32),
+            pltpu.VMEM((kv_local, 2, samples, block_rows * heads, DH), BF16),
+            pltpu.VMEM((kv_local, 2, block_rows * heads, DH), BF16),
+            pltpu.VMEM((kv_local, 2, heads, block_rows, DH), BF16),
+            pltpu.VMEM((peers, block_rows, DH), BF16),
+            pltpu.VMEM(queries.shape, BF16),
+            pltpu.VMEM(queries.shape, BF16),
+            pltpu.SemaphoreType.DMA((2,)),
             pltpu.SemaphoreType.DMA((kv_local, 2, peers)),
             pltpu.SemaphoreType.DMA((kv_local, 2, peers)),
-            pltpu.SemaphoreType.DMA((kv_local, 2, peers)),
-            pltpu.SemaphoreType.DMA((kv_local, 2, peers)),
+            pltpu.SemaphoreType.DMA((peers,)),
+            pltpu.SemaphoreType.DMA((peers,)),
+            pltpu.SemaphoreType.DMA((kv_local, 2, samples)),
+            pltpu.SemaphoreType.DMA((kv_local, 2, samples)),
+            pltpu.SemaphoreType.DMA((kv_local, 2, heads)),
+            pltpu.SemaphoreType.DMA((kv_local, 2, heads)),
         ],
         compiler_params=pltpu.CompilerParams(
-            collective_id=0, has_side_effects=True, vmem_limit_bytes=60 * 1024 * 1024
+            collective_id=0, has_side_effects=True, vmem_limit_bytes=58 * 1024 * 1024
         ),
     )(prompt_len, comp_len, queries, grad_out, kv_comp, kv_prefix)
     return pl.pallas_call(
         write_out,
         out_shape=tuple(jax.ShapeDtypeStruct(shape, BF16) for shape in shapes),
-        in_specs=[pl.BlockSpec(memory_space=pl.ANY)] * 4,
-        out_specs=(pl.BlockSpec(memory_space=pl.ANY),) * 4,
+        in_specs=[hbm] * 4,
+        out_specs=(hbm,) * 4,
         scratch_shapes=[pltpu.SemaphoreType.DMA((4,))],
         compiler_params=pltpu.CompilerParams(vmem_limit_bytes=1024 * 1024),
     )(*results)

time: 35.6 us -> 33.7 us (0.947)
  Pallas kernels: 34.1 us -> 32.2 us
    pallas_call x1, Pallas kernels: 32.6 us -> 30.7 us  [body(): pl.pallas_call(functools.partial(kernel, samples, heads), out_shape=tuple...]
where the time goes in v4:
time: 33.7 us; the launch traced here: 33.5 us
  Pallas kernels  32.2 us (96%)
  between operations  1.29 us (4%)
    pallas_call x1, Pallas kernels, body(): pl.pallas_call(functools.partial(kernel, samples, heads), out_shape=tuple...  30.7 us
    pallas_call x1, Pallas kernels, body(): pl.pallas_call(write_out, out_shape=tuple((jax.ShapeDtypeStruct(shape, BF...  1.52 us

profile of v4, /device:TPU:0, one launch (start us, length us, event | category | flops | bytes accessed | tf_op | source)
XLA Modules:
  0.0 33.5 jit_solution(14828105628033805554)
XLA Ops:
  1.3 30.7 %shard_map.93 = (bf16[1,2,128,2048]{3,2,1,0:T(8,128)(2,1)S(1)}, bf16[1,2,128,2048]{3,2,1,0:T(8,128)(2,1)S(1)}, bf16[2,1,2,128,256]{4,3,2,1,0:T(8,128)(2,1)S(1)}, bf16[2,1,64,1024]{3,2,1,0:T(8,128)(2,1)S(1)}) custom-call(s32[1]{0:T(128)S(6)} %copy.10.plen_ref, s32[1,2]{1,0:T(1,128)} %clen_ref.1, bf16[1,2,128,2048]{3,2,1,0:T(8,128)(2,1)} %q_any.1, ...), custom_call_target="tpu_custom_call" | custom-call | tf_op jit(solution)/shard_map/pallas_call | solution.py:370
  32.0 1.5 %shard_map.94 = (bf16[1,2,128,2048]{3,2,1,0:T(8,128)(2,1)}, bf16[1,2,128,2048]{3,2,1,0:T(8,128)(2,1)}, bf16[2,1,2,128,256]{4,3,2,1,0:T(8,128)(2,1)}, bf16[2,1,64,1024]{3,2,1,0:T(8,128)(2,1)}) custom-call(bf16[1,2,128,2048]{3,2,1,0:T(8,128)(2,1)S(1)} %get-tuple-element.8.refs_0_, bf16[1,2,128,2048]{3,2,1,0:T(8,128)(2,1)S(1)} %get-tuple-element.9.refs_1_, ...), custom_call_target="tpu_custom_call" | custom-call | tf_op jit(solution)/shard_map/pallas_call | solution.py:407
